TPU v7x, 32 devices: a whole 2x2x4 slice. The times are simulated.
32 devices in a mesh: group: 2 (over x), cell: 16 (over z, y, core).
Axes of the slice: x: 2, y: 2, z: 4, core: 2. Of those that a mesh axis runs over, the one named last changes fastest.
Arguments:
- adjoint_seed: float32 [32, 5, 16384], P('group', None, 'cell'), parts along dimension 0, may hold values from -6 to 6
- inv_blocks: bfloat16 [32, 5, 5, 16384], P('group', None, None, 'cell'), parts along dimension 0
- flux_jacobians: float32 [2, 32, 5, 5], P(None, 'group'), parts along dimension 1, may hold values from -1.5 to 1.5
- modal_shapes: float32 [20, 5, 16384], P(None, None, 'cell'), may hold values from -0.01953125 to 0.01953125
- modal_gain: float32 [40], P('group'), parts along dimension 0, may hold values from 0.05 to 0.3
- face_cells: int32 [2, 49152], P(None, 'cell'), may hold values from 0 to 1279, as said below
- face_weights: float32 [49152], P('cell'), may hold values from 0.4 to 1
- colours: int32 [16384], P('cell'), may hold values from 0 to 1
- send_cells: int32 [2, 2048], P(None, 'cell'), may hold values from 0 to 1023, as said below
Outputs:
- adjoint_state: float32 [32, 5, 16384], P('group', None, 'cell'), parts along dimension 0
- modal_partials: float32 [32, 20], P('group'), parts along dimension 0
There are 2 independent parts, one for each index of `group`. A program takes and returns all parts, laid end to end along the dimension named above; an argument that names none is the same for every part. Nothing has to cross between parts.
Inputs may be any that keep to these rules, and one draw needn't show every extreme that they name: `face_cells`: each face's left cell is a local cell or a lower ghost (from 1024 to 1151); its right cell is a local cell or an upper ghost (from 1152 on). `send_cells`: within a partition the 256 listed cells are distinct local cells.
All inputs are finite; a program needn't handle non-finite values.
Results may differ from a plain program's by a relative error of at most 0.0003.
Values sent between devices are 32-bit elements; how exact they have to be, the bound alone decides.
A program may use at most 64 MiB of HBM per device.

v0:
```python
import math
import jax
import jax.numpy as jnp
import numpy as np
from jax import lax
from jax.sharding import PartitionSpec as P

ITERS = 4
frequency = 0.04


def from_behind(value, axis, by):
    devices = lax.axis_size(axis)
    return lax.ppermute(value, axis, [(i, (i + by) % devices) for i in range(devices)])


def spectral_matrix(count):
    index = jnp.arange(count)
    apart = index[:, None] - index[None, :]
    angle = math.pi * apart.astype(jnp.float32) / count
    parity = jnp.where(apart % 2 == 0, 1.0, -1.0).astype(jnp.float32)
    safe_sin = jnp.where(apart == 0, 1.0, jnp.sin(angle))
    return jnp.where(apart == 0, 0.0, 0.5 * parity * jnp.cos(angle) / safe_sin)


def wide_dot(left, right):
    return jnp.dot(left, right, precision=lax.Precision.HIGHEST, preferred_element_type=jnp.float32)


def modal_total(state_rows, shape_rows, count, nvar, modes):
    gram = lax.dot_general(
        state_rows,
        shape_rows,
        (((1,), (1,)), ((), ())),
        precision=lax.Precision.HIGHEST,
        preferred_element_type=jnp.float32,
    )
    local_part = jnp.einsum("ivmv->im", gram.reshape(count, nvar, modes, nvar))
    return lax.psum(local_part, "cell")


def local(
    adjoint_seed,
    inv_blocks,
    flux_jacobians,
    modal_shapes,
    modal_gain,
    face_cells,
    face_weights,
    colours,
    send_cells,
):
    count, nvar, owned = adjoint_seed.shape
    modes = modal_shapes.shape[0]
    rows = count * nvar
    eye_inst = jnp.eye(count, dtype=jnp.float32)
    eye_var = jnp.eye(nvar, dtype=jnp.float32)
    left_matrix = jnp.einsum("ij,ivw->iwjv", eye_inst, flux_jacobians[0]).reshape(rows, rows)
    right_matrix = jnp.einsum("ij,ivw->iwjv", eye_inst, flux_jacobians[1]).reshape(rows, rows)
    spectral = spectral_matrix(count)
    spectral_rows = frequency * jnp.einsum("jk,vu->kvju", spectral, eye_var).reshape(rows, rows)
    seed_rows = adjoint_seed.reshape(rows, owned)
    shape_rows = modal_shapes.reshape(modes * nvar, owned)
    flat_inverse = inv_blocks.reshape(count * nvar * nvar, owned)
    inst_index = np.arange(count)[:, None]
    out_index = np.arange(nvar)[None, :]
    inverse_parts = []
    source_rows = []
    for var in range(nvar):
        pick = (inst_index * nvar * nvar + var * nvar + out_index).reshape(-1)
        inverse_parts.append(
            jnp.take(flat_inverse, jnp.asarray(pick, jnp.int32), axis=0).astype(jnp.float32)
        )
        source_rows.append(
            jnp.asarray((inst_index * nvar + var + 0 * out_index).reshape(-1), jnp.int32)
        )
    left_cells = face_cells[0]
    right_cells = face_cells[1]
    colour_mask = colours[None, :]
    state = jnp.zeros_like(seed_rows)
    for sweep in range(ITERS):
        lam = modal_total(state, shape_rows, count, nvar, modes) * modal_gain[None, :]
        lift = jnp.einsum("im,vu->ivmu", lam, eye_var).reshape(rows, modes * nvar)
        base = seed_rows + wide_dot(lift, shape_rows)
        to_lower = jnp.take(state, send_cells[0], axis=1)
        to_upper = jnp.take(state, send_cells[1], axis=1)
        from_lower = from_behind(to_upper, "cell", 1)
        from_upper = from_behind(to_lower, "cell", -1)
        ghosts = jnp.concatenate([from_lower, from_upper], axis=1)
        for colour in range(2):
            extended = jnp.concatenate([state, ghosts], axis=1)
            from_left = wide_dot(left_matrix, extended)
            from_right = wide_dot(right_matrix, extended)
            total = jnp.zeros_like(extended)
            total = total.at[:, right_cells].add(
                face_weights * jnp.take(from_left, left_cells, axis=1)
            )
            total = total.at[:, left_cells].add(
                face_weights * jnp.take(from_right, right_cells, axis=1)
            )
            spectral_term = wide_dot(spectral_rows, state)
            resid = base - total[:, :owned] - spectral_term
            updated = inverse_parts[0] * jnp.take(resid, source_rows[0], axis=0)
            for var in range(1, nvar):
                updated = updated + inverse_parts[var] * jnp.take(resid, source_rows[var], axis=0)
            state = jnp.where(colour_mask == colour, updated, state)
    partials = modal_total(state, shape_rows, count, nvar, modes)
    return (state.reshape(count, nvar, owned), partials)


def solution(mesh):
    return jax.shard_map(
        local,
        mesh=mesh,
        in_specs=(
            P("group", None, "cell"),
            P("group", None, None, "cell"),
            P(None, "group", None, None),
            P(None, None, "cell"),
            P("group"),
            P(None, "cell"),
            P("cell"),
            P("cell"),
            P(None, "cell"),
        ),
        out_specs=(P("group", None, "cell"), P("group", None)),
        check_vma=False,
    )
```

profile of v0, /device:TPU:0, one launch (start us, length us, event | category | flops | bytes accessed | tf_op | source)
XLA Modules:
  0.0 821.3 jit_solution(13111969591882598238)
XLA Ops:
  2.9 5.4 collective-permute-start.1
  12.7 34.5 %psum.35 = f32[16,20]{1,0:T(8,128)S(1)} all-reduce(f32[16,20]{1,0:T(8,128)S(1)} %fusion.48), channel_id=1, replica_groups=mesh['group'=2,'cell'=16] {'cell'}, use_global_device_ids=true, to_apply=%region_1.3 | all-reduce | flops 320 | bytes 2560 | tf_op jit(solution)/shard_map/psum | solution.py:39
  65.2 26.8 %scatter_custom_fusion = f32[80,1280]{0,1:T(8,128)} fusion(s32[3072]{0:T(1024)} %bitcast.273, f32[]{:T(128)} %constant.24.clone.8, f32[3072]{0:T(1024)S(1)} %copy-done.1, pred[3072]{0:T(1024)(128)(4,1)S(1)} %compare_and_fusion, f32[]{:T(128)} %constant.44.clone.1, f32[80,1280]{0,1:T(8,128)S(1)} %fusion.107, s32[3072]{0:T(1024)S(1)} %fusion.178), kind=kCustom, calls=%fused_computation.130 | custom fusion | flops 737280 | bytes 847872 | tf_op jit(solution)/shard_map/scatter-add | solution.py:95
  94.0 27.7 %scatter_custom_fusion.1 = f32[80,1280]{0,1:T(8,128)} fusion(f32[80,1280]{0,1:T(8,128)} %scatter_custom_fusion, s32[3072]{0:T(1024)} %bitcast.265, f32[]{:T(128)} %constant.24.clone.8, f32[3072]{0:T(1024)S(1)} %copy-done.1, pred[3072]{0:T(1024)(128)(4,1)S(1)} %compare_and_fusion.1, f32[80,1280]{0,1:T(8,128)S(1)} %fusion.106, s32[3072]{0:T(1024)S(1)} %fusion.177), kind=kCustom, calls=%fused_computation.127 | custom fusion | flops 737280 | bytes 847360 | tf_op jit(solution)/shard_map/scatter-add | solution.py:98
  132.2 26.8 %scatter_custom_fusion.2 = f32[80,1280]{0,1:T(8,128)} fusion(s32[3072]{0:T(1024)} %bitcast.274, f32[]{:T(128)} %constant.24.clone.8, f32[3072]{0:T(1024)S(1)} %copy-done.1, pred[3072]{0:T(1024)(128)(4,1)S(1)} %compare_and_fusion, f32[]{:T(128)} %constant.44.clone.1, f32[80,1280]{0,1:T(8,128)S(1)} %fusion.174, s32[3072]{0:T(1024)S(1)} %fusion.178), kind=kCustom, calls=%fused_computation.124 | custom fusion | flops 737280 | bytes 847872 | tf_op jit(solution)/shard_map/scatter-add | solution.py:95
  161.0 27.7 %scatter_custom_fusion.3 = f32[80,1280]{0,1:T(8,128)} fusion(f32[80,1280]{0,1:T(8,128)} %scatter_custom_fusion.2, s32[3072]{0:T(1024)} %bitcast.266, f32[]{:T(128)} %constant.24.clone.8, f32[3072]{0:T(1024)S(1)} %copy-done.1, pred[3072]{0:T(1024)(128)(4,1)S(1)} %compare_and_fusion.1, f32[80,1280]{0,1:T(8,128)S(1)} %fusion.173, s32[3072]{0:T(1024)S(1)} %fusion.177), kind=kCustom, calls=%fused_computation.121 | custom fusion | flops 737280 | bytes 847360 | tf_op jit(solution)/shard_map/scatter-add | solution.py:98
  206.5 30.0 %psum.36 = f32[16,20]{1,0:T(8,128)S(1)} all-reduce(f32[16,20]{1,0:T(8,128)S(1)} %fusion.49), channel_id=1, replica_groups=mesh['group'=2,'cell'=16] {'cell'}, use_global_device_ids=true, to_apply=%region_7.12 | all-reduce | flops 320 | bytes 2560 | tf_op jit(solution)/shard_map/psum | solution.py:39
  240.9 4.4 collective-permute-done.2
  247.9 26.6 %scatter_custom_fusion.4 = f32[80,1280]{0,1:T(8,128)} fusion(s32[3072]{0:T(1024)} %bitcast.275, f32[]{:T(128)} %constant.24.clone.8, f32[3072]{0:T(1024)S(1)} %copy-done.1, pred[3072]{0:T(1024)(128)(4,1)S(1)} %compare_and_fusion, f32[]{:T(128)} %constant.44.clone.1, f32[80,1280]{0,1:T(8,128)S(1)} %fusion.170, s32[3072]{0:T(1024)S(1)} %fusion.178), kind=kCustom, calls=%fused_computation.118 | custom fusion | flops 737280 | bytes 847872 | tf_op jit(solution)/shard_map/scatter-add | solution.py:95
  276.6 27.8 %scatter_custom_fusion.5 = f32[80,1280]{0,1:T(8,128)} fusion(f32[80,1280]{0,1:T(8,128)} %scatter_custom_fusion.4, s32[3072]{0:T(1024)} %bitcast.267, f32[]{:T(128)} %constant.24.clone.8, f32[3072]{0:T(1024)S(1)} %copy-done.1, pred[3072]{0:T(1024)(128)(4,1)S(1)} %compare_and_fusion.1, f32[80,1280]{0,1:T(8,128)S(1)} %fusion.169, s32[3072]{0:T(1024)S(1)} %fusion.177), kind=kCustom, calls=%fused_computation.115 | custom fusion | flops 737280 | bytes 847360 | tf_op jit(solution)/shard_map/scatter-add | solution.py:98
  318.5 37.3 %scatter_custom_fusion.6 = f32[80,1280]{0,1:T(8,128)} fusion(s32[3072]{0:T(1024)} %bitcast.276, f32[]{:T(128)} %constant.24.clone.8, f32[3072]{0:T(1024)S(1)} %copy-done.1, pred[3072]{0:T(1024)(128)(4,1)S(1)} %compare_and_fusion, f32[]{:T(128)} %constant.44.clone.1, f32[80,1280]{0,1:T(8,128)} %fusion.172, s32[3072]{0:T(1024)S(1)} %fusion.178), kind=kCustom, calls=%fused_computation.112 | custom fusion | flops 737280 | bytes 1093632 | tf_op jit(solution)/shard_map/scatter-add | solution.py:95
  357.9 38.6 %scatter_custom_fusion.7 = f32[80,1280]{0,1:T(8,128)} fusion(f32[80,1280]{0,1:T(8,128)} %scatter_custom_fusion.6, s32[3072]{0:T(1024)} %bitcast.268, f32[]{:T(128)} %constant.24.clone.8, f32[3072]{0:T(1024)S(1)} %copy-done.1, pred[3072]{0:T(1024)(128)(4,1)S(1)} %compare_and_fusion.1, f32[80,1280]{0,1:T(8,128)} %fusion.171, s32[3072]{0:T(1024)S(1)} %fusion.177), kind=kCustom, calls=%fused_computation.109 | custom fusion | flops 737280 | bytes 1093120 | tf_op jit(solution)/shard_map/scatter-add | solution.py:98
  413.6 30.0 %psum.37 = f32[16,20]{1,0:T(8,128)S(1)} all-reduce(f32[16,20]{1,0:T(8,128)S(1)} %fusion.50), channel_id=1, replica_groups=mesh['group'=2,'cell'=16] {'cell'}, use_global_device_ids=true, to_apply=%region_13.18 | all-reduce | flops 320 | bytes 2560 | tf_op jit(solution)/shard_map/psum | solution.py:39
  454.7 27.0 %scatter_custom_fusion.8 = f32[80,1280]{0,1:T(8,128)} fusion(s32[3072]{0:T(1024)} %bitcast.277, f32[]{:T(128)} %constant.24.clone.8, f32[3072]{0:T(1024)S(1)} %copy-done.1, pred[3072]{0:T(1024)(128)(4,1)S(1)} %compare_and_fusion, f32[]{:T(128)} %constant.44.clone.1, f32[80,1280]{0,1:T(8,128)S(1)} %fusion.166, s32[3072]{0:T(1024)S(1)} %fusion.178), kind=kCustom, calls=%fused_computation.106 | custom fusion | flops 737280 | bytes 847872 | tf_op jit(solution)/shard_map/scatter-add | solution.py:95
  483.7 27.7 %scatter_custom_fusion.9 = f32[80,1280]{0,1:T(8,128)} fusion(f32[80,1280]{0,1:T(8,128)} %scatter_custom_fusion.8, s32[3072]{0:T(1024)} %bitcast.269, f32[]{:T(128)} %constant.24.clone.8, f32[3072]{0:T(1024)S(1)} %copy-done.1, pred[3072]{0:T(1024)(128)(4,1)S(1)} %compare_and_fusion.1, f32[80,1280]{0,1:T(8,128)S(1)} %fusion.165, s32[3072]{0:T(1024)S(1)} %fusion.177), kind=kCustom, calls=%fused_computation.103 | custom fusion | flops 737280 | bytes 847360 | tf_op jit(solution)/shard_map/scatter-add | solution.py:98
  525.5 37.5 %scatter_custom_fusion.10 = f32[80,1280]{0,1:T(8,128)} fusion(s32[3072]{0:T(1024)} %bitcast.278, f32[]{:T(128)} %constant.24.clone.8, f32[3072]{0:T(1024)S(1)} %copy-done.1, pred[3072]{0:T(1024)(128)(4,1)S(1)} %compare_and_fusion, f32[]{:T(128)} %constant.44.clone.1, f32[80,1280]{0,1:T(8,128)} %fusion.168, s32[3072]{0:T(1024)S(1)} %fusion.178), kind=kCustom, calls=%fused_computation.100 | custom fusion | flops 737280 | bytes 1093632 | tf_op jit(solution)/shard_map/scatter-add | solution.py:95
  565.0 38.4 %scatter_custom_fusion.11 = f32[80,1280]{0,1:T(8,128)} fusion(f32[80,1280]{0,1:T(8,128)} %scatter_custom_fusion.10, s32[3072]{0:T(1024)} %bitcast.270, f32[]{:T(128)} %constant.24.clone.8, f32[3072]{0:T(1024)S(1)} %copy-done.1, pred[3072]{0:T(1024)(128)(4,1)S(1)} %compare_and_fusion.1, f32[80,1280]{0,1:T(8,128)} %fusion.167, s32[3072]{0:T(1024)S(1)} %fusion.177), kind=kCustom, calls=%fused_computation.97 | custom fusion | flops 737280 | bytes 1093120 | tf_op jit(solution)/shard_map/scatter-add | solution.py:98
  620.5 30.4 %psum.38 = f32[16,20]{1,0:T(8,128)S(1)} all-reduce(f32[16,20]{1,0:T(8,128)S(1)} %fusion.51), channel_id=1, replica_groups=mesh['group'=2,'cell'=16] {'cell'}, use_global_device_ids=true, to_apply=%region_19.24 | all-reduce | flops 320 | bytes 2560 | tf_op jit(solution)/shard_map/psum | solution.py:39
  654.8 4.8 collective-permute-done.6
  661.5 26.0 %scatter_custom_fusion.12 = f32[80,1280]{0,1:T(8,128)S(1)} fusion(s32[3072]{0:T(1024)} %bitcast.279, f32[]{:T(128)} %constant.24.clone.8, f32[3072]{0:T(1024)S(1)} %copy-done.1, pred[3072]{0:T(1024)(128)(4,1)S(1)} %compare_and_fusion, f32[]{:T(128)} %constant.44.clone.1, f32[80,1280]{0,1:T(8,128)S(1)} %fusion.162, s32[3072]{0:T(1024)S(1)} %fusion.178), kind=kCustom, calls=%fused_computation.94 | custom fusion | flops 737280 | bytes 847872 | tf_op jit(solution)/shard_map/scatter-add | solution.py:95
  688.7 26.3 %scatter_custom_fusion.13 = f32[80,1280]{0,1:T(8,128)S(1)} fusion(f32[80,1280]{0,1:T(8,128)S(1)} %scatter_custom_fusion.12, s32[3072]{0:T(1024)} %bitcast.271, f32[]{:T(128)} %constant.24.clone.8, f32[3072]{0:T(1024)S(1)} %copy-done.1, pred[3072]{0:T(1024)(128)(4,1)S(1)} %compare_and_fusion.1, f32[80,1280]{0,1:T(8,128)S(1)} %fusion.161, s32[3072]{0:T(1024)S(1)} %fusion.177), kind=kCustom, calls=%fused_computation.91 | custom fusion | flops 737280 | bytes 1093120 | tf_op jit(solution)/shard_map/scatter-add | solution.py:98
  723.8 26.6 %scatter_custom_fusion.14 = f32[80,1280]{0,1:T(8,128)} fusion(s32[3072]{0:T(1024)} %bitcast.280, f32[]{:T(128)} %constant.24.clone.8, f32[3072]{0:T(1024)S(1)} %copy-done.1, pred[3072]{0:T(1024)(128)(4,1)S(1)} %compare_and_fusion, f32[]{:T(128)} %constant.44.clone.1, f32[80,1280]{0,1:T(8,128)S(1)} %fusion.164, s32[3072]{0:T(1024)S(1)} %fusion.178), kind=kCustom, calls=%fused_computation.88 | custom fusion | flops 737280 | bytes 847872 | tf_op jit(solution)/shard_map/scatter-add | solution.py:95
  751.6 27.9 %scatter_custom_fusion.15 = f32[80,1280]{0,1:T(8,128)} fusion(f32[80,1280]{0,1:T(8,128)} %scatter_custom_fusion.14, s32[3072]{0:T(1024)} %bitcast.272, f32[]{:T(128)} %constant.24.clone.8, f32[3072]{0:T(1024)S(1)} %copy-done.1, pred[3072]{0:T(1024)(128)(4,1)S(1)} %compare_and_fusion.1, f32[80,1280]{0,1:T(8,128)S(1)} %fusion.163, s32[3072]{0:T(1024)S(1)} %fusion.177), kind=kCustom, calls=%fused_computation.85 | custom fusion | flops 737280 | bytes 847360 | tf_op jit(solution)/shard_map/scatter-add | solution.py:98
  790.0 30.8 %psum.39 = f32[16,20]{1,0:T(8,128)} all-reduce(f32[16,20]{1,0:T(8,128)S(1)} %fusion.52), channel_id=1, replica_groups=mesh['group'=2,'cell'=16] {'cell'}, use_global_device_ids=true, to_apply=%region_25.30 | all-reduce | flops 320 | bytes 2560 | tf_op jit(solution)/shard_map/psum | solution.py:39
  (310 shorter events, 171.9 us)
Async XLA Ops:
  0.6 9.1 %copy-start.24 = (s32[2,3072]{1,0:T(2,128)S(1)}, s32[2,3072]{1,0:T(2,128)}, u32[]{:S(2)}) copy-start(s32[2,3072]{1,0:T(2,128)} %param.32) | copy-start | bytes 73732
  0.6 10.0 %copy-start.23 = (f32[16,5,1024]{2,0,1:T(8,128)S(1)}, f32[16,5,1024]{2,0,1:T(8,128)}, u32[]{:S(2)}) copy-start(f32[16,5,1024]{2,0,1:T(8,128)} %param.27) | copy-start | bytes 983044
  2.2 8.7 %copy-start = (f32[20,5,1024]{2,0,1:T(8,128)S(1)}, f32[20,5,1024]{2,0,1:T(8,128)}, u32[]{:S(2)}) copy-start(f32[20,5,1024]{2,0,1:T(8,128)} %param.30) | copy-start | bytes 1228804
  2.9 59.0 %collective-permute-start.1 = (f32[80,128]{1,0:T(8,128)}, f32[80,128]{1,0:T(8,128)S(1)}, u32[]{:S(2)}, u32[]{:S(2)}) collective-permute-start(f32[80,128]{1,0:T(8,128)} %select_bitcast_fusion.6), channel_id=1, source_target_pairs={{0,15},{1,0},{2,1},{3,2},{4,3},{5,4},{6,5},{7,6},{8,7},{9,8},{10,9... | collective-permute-start | bytes 122888 | tf_op jit(solution)/shard_map/ppermute | solution.py:14
  9.7 52.2 %collective-permute-start = (f32[80,128]{1,0:T(8,128)}, f32[80,128]{1,0:T(8,128)S(1)}, u32[]{:S(2)}, u32[]{:S(2)}) collective-permute-start(f32[80,128]{1,0:T(8,128)} %select_bitcast_fusion.7), channel_id=1, source_target_pairs={{0,1},{1,2},{2,3},{3,4},{4,5},{5,6},{6,7},{7,8},{8,9},{9,10},{10,1... | collective-permute-start | bytes 122888 | tf_op jit(solution)/shard_map/ppermute | solution.py:14
  10.8 36.4 %copy-start.38 = (f32[20]{0:T(128)S(1)}, f32[20]{0:T(128)}, u32[]{:S(2)}) copy-start(f32[20]{0:T(128)} %param.31) | copy-start | bytes 244
  201.5 35.0 %copy-start.39 = (f32[20]{0:T(128)S(1)}, f32[20]{0:T(128)}, u32[]{:S(2)}) copy-start(f32[20]{0:T(128)} %param.31) | copy-start | bytes 244
  203.8 34.9 %copy-start.32 = (pred[128]{0:T(512)(128)(4,1)S(1)}, pred[128]{0:T(512)(128)(4,1)}, u32[]{:S(2)}) copy-start(pred[128]{0:T(512)(128)(4,1)} %copy-done.31) | copy-start | bytes 388
  238.6 1.7 collective-permute-start.3
  238.8 6.6 collective-permute-start.2
  316.4 39.4 %copy-start.13 = (f32[80,128]{1,0:T(8,128)S(1)}, f32[80,128]{1,0:T(8,128)}, u32[]{:S(2)}) copy-start(f32[80,128]{1,0:T(8,128)} %copy-done.11) | copy-start | bytes 122884
  316.4 39.4 %copy-start.19 = (f32[80,128]{1,0:T(8,128)S(1)}, f32[80,128]{1,0:T(8,128)}, u32[]{:S(2)}) copy-start(f32[80,128]{1,0:T(8,128)} %copy-done.17) | copy-start | bytes 122884
  408.6 35.0 %copy-start.40 = (f32[20]{0:T(128)S(1)}, f32[20]{0:T(128)}, u32[]{:S(2)}) copy-start(f32[20]{0:T(128)} %param.31) | copy-start | bytes 244
  411.0 34.9 %copy-start.33 = (pred[128]{0:T(512)(128)(4,1)S(1)}, pred[128]{0:T(512)(128)(4,1)}, u32[]{:S(2)}) copy-start(pred[128]{0:T(512)(128)(4,1)} %copy-done.31) | copy-start | bytes 388
  445.8 1.7 collective-permute-start.5
  445.9 6.2 collective-permute-start.4
  523.4 39.5 %copy-start.16 = (f32[80,128]{1,0:T(8,128)S(1)}, f32[80,128]{1,0:T(8,128)}, u32[]{:S(2)}) copy-start(f32[80,128]{1,0:T(8,128)} %copy-done.14) | copy-start | bytes 122884
  523.4 39.5 %copy-start.22 = (f32[80,128]{1,0:T(8,128)S(1)}, f32[80,128]{1,0:T(8,128)}, u32[]{:S(2)}) copy-start(f32[80,128]{1,0:T(8,128)} %copy-done.20) | copy-start | bytes 122884
  615.5 35.4 %copy-start.41 = (f32[20]{0:T(128)S(1)}, f32[20]{0:T(128)}, u32[]{:S(2)}) copy-start(f32[20]{0:T(128)} %param.31) | copy-start | bytes 244
  617.9 35.3 %copy-start.34 = (pred[128]{0:T(512)(128)(4,1)S(1)}, pred[128]{0:T(512)(128)(4,1)}, u32[]{:S(2)}) copy-start(pred[128]{0:T(512)(128)(4,1)} %copy-done.31) | copy-start | bytes 388
  653.1 1.7 collective-permute-start.7
  653.2 6.4 collective-permute-start.6
  661.4 26.0 %copy-start.8 = (f32[80,128]{1,0:T(8,128)S(1)}, f32[80,128]{1,0:T(8,128)}, u32[]{:S(2)}) copy-start(f32[80,128]{1,0:T(8,128)} %copy-done.7) | copy-start | bytes 122884
  661.5 26.0 %copy-start.10 = (f32[80,128]{1,0:T(8,128)S(1)}, f32[80,128]{1,0:T(8,128)}, u32[]{:S(2)}) copy-start(f32[80,128]{1,0:T(8,128)} %copy-done.9) | copy-start | bytes 122884
  (37 other events, 87.0 us)
where the time goes:
time: 833 us; the launch traced here: 821 us
  other arithmetic  498 us (60%)
  blocking collectives  156 us (19%)
  local copies, waits for them, and re-layouts  96.2 us (12%)
  matrix products  47.3 us (6%)
  waiting for transfers between devices  14.2 us (2%)
    scatter-add x8, other arithmetic, local(): total.at[:, left_cells]  242 us
    scatter-add x8, other arithmetic, local(): total.at[:, right_cells]  235 us
    psum x5, blocking collectives, modal_total(): return lax.psum(local_part, 'cell')  156 us
    gather x32, local copies, waits for them, and re-layouts, local(): jnp.take(resid, source_rows[var], axis=0)  43.6 us
    dot_general x28, matrix products, wide_dot(): jnp.dot(left, right, precision=lax.Precision.HIGHEST, preferred_element_t...  36.4 us
  transfers between devices with their start and end apart: 8, of which 6 were waited for; matrix products, arithmetic and copies ran while one was open for 2% of the time, Pallas kernels for 0%

commit v1 on v0

--- a/solution.py
+++ b/solution.py
@@ -36,7 +36,7 @@
         preferred_element_type=jnp.float32,
     )
     local_part = jnp.einsum("ivmv->im", gram.reshape(count, nvar, modes, nvar))
-    return lax.psum(local_part, "cell")
+    return jnp.sum(lax.all_gather(local_part, "cell"), axis=0)
 
 
 def local(

time: 833 us -> 772 us (0.927)
  blocking collectives: 156 us -> 89.5 us
    psum x5 -> x0, blocking collectives: 156 us -> none  [modal_total(): return lax.psum(local_part, 'cell')]
    all_gather x0 -> x5, blocking collectives: none -> 89.5 us  [modal_total(): return jnp.sum(lax.all_gather(local_part, 'cell'), axis=0)]
  transfers between devices with their start and end apart: 8 -> 8, of which waited for: 6 -> 6; matrix products, arithmetic and copies ran while one was open for 2% -> 3% of each run, Pallas kernels for 0% -> 0%
where the time goes in v1:
time: 772 us; the launch traced here: 760 us
  other arithmetic  498 us (65%)
  local copies, waits for them, and re-layouts  96.2 us (12%)
  blocking collectives  89.5 us (12%)
  matrix products  47.3 us (6%)
  waiting for transfers between devices  15.7 us (2%)
  starting transfers between devices  11 us (1%)
    scatter-add x8, other arithmetic, local(): total.at[:, left_cells]  242 us
    scatter-add x8, other arithmetic, local(): total.at[:, right_cells]  235 us
    all_gather x5, blocking collectives, modal_total(): return jnp.sum(lax.all_gather(local_part, 'cell'), axis=0)  89.5 us
    gather x32, local copies, waits for them, and re-layouts, local(): jnp.take(resid, source_rows[var], axis=0)  43.6 us
    dot_general x28, matrix products, wide_dot(): jnp.dot(left, right, precision=lax.Precision.HIGHEST, preferred_element_t...  36.4 us
    ppermute x8, waiting for transfers between devices, from_behind(): lax.ppermute(value, axis, [(i, (i + by) % devices) for i in range(devices)])  15.7 us
  transfers between devices with their start and end apart: 8, of which 6 were waited for; matrix products, arithmetic and copies ran while one was open for 3% of the time, Pallas kernels for 0%

profile of v1, /device:TPU:0, one launch (start us, length us, event | category | flops | bytes accessed | tf_op | source)
XLA Modules:
  0.0 760.4 jit_solution(7187127222050761681)
XLA Ops:
  2.9 5.4 collective-permute-start.1
  12.7 18.5 %all-gather = f32[256,20]{1,0:T(8,128)S(1)} all-gather(f32[16,20]{1,0:T(8,128)S(1)} %fusion.48), channel_id=2, replica_groups=mesh['group'=2,'cell'=16] {'cell'}, dimensions={0}, use_global_device_ids=true | all-gather | bytes 21760 | tf_op jit(solution)/shard_map/all_gather | solution.py:39
  49.2 26.8 %scatter_custom_fusion = f32[80,1280]{0,1:T(8,128)} fusion(s32[3072]{0:T(1024)} %bitcast.283, f32[]{:T(128)} %constant.24.clone.8, f32[3072]{0:T(1024)S(1)} %copy-done.1, pred[3072]{0:T(1024)(128)(4,1)S(1)} %compare_and_fusion, f32[]{:T(128)} %constant.44.clone.1, f32[80,1280]{0,1:T(8,128)S(1)} %fusion.107, s32[3072]{0:T(1024)S(1)} %fusion.178), kind=kCustom, calls=%fused_computation.130 | custom fusion | flops 737280 | bytes 847872 | tf_op jit(solution)/shard_map/scatter-add | solution.py:95
  78.0 27.7 %scatter_custom_fusion.1 = f32[80,1280]{0,1:T(8,128)} fusion(f32[80,1280]{0,1:T(8,128)} %scatter_custom_fusion, s32[3072]{0:T(1024)} %bitcast.275, f32[]{:T(128)} %constant.24.clone.8, f32[3072]{0:T(1024)S(1)} %copy-done.1, pred[3072]{0:T(1024)(128)(4,1)S(1)} %compare_and_fusion.1, f32[80,1280]{0,1:T(8,128)S(1)} %fusion.106, s32[3072]{0:T(1024)S(1)} %fusion.177), kind=kCustom, calls=%fused_computation.127 | custom fusion | flops 737280 | bytes 847360 | tf_op jit(solution)/shard_map/scatter-add | solution.py:98
  116.2 26.8 %scatter_custom_fusion.2 = f32[80,1280]{0,1:T(8,128)} fusion(s32[3072]{0:T(1024)} %bitcast.284, f32[]{:T(128)} %constant.24.clone.8, f32[3072]{0:T(1024)S(1)} %copy-done.1, pred[3072]{0:T(1024)(128)(4,1)S(1)} %compare_and_fusion, f32[]{:T(128)} %constant.44.clone.1, f32[80,1280]{0,1:T(8,128)S(1)} %fusion.174, s32[3072]{0:T(1024)S(1)} %fusion.178), kind=kCustom, calls=%fused_computation.124 | custom fusion | flops 737280 | bytes 847872 | tf_op jit(solution)/shard_map/scatter-add | solution.py:95
  145.0 27.7 %scatter_custom_fusion.3 = f32[80,1280]{0,1:T(8,128)} fusion(f32[80,1280]{0,1:T(8,128)} %scatter_custom_fusion.2, s32[3072]{0:T(1024)} %bitcast.276, f32[]{:T(128)} %constant.24.clone.8, f32[3072]{0:T(1024)S(1)} %copy-done.1, pred[3072]{0:T(1024)(128)(4,1)S(1)} %compare_and_fusion.1, f32[80,1280]{0,1:T(8,128)S(1)} %fusion.173, s32[3072]{0:T(1024)S(1)} %fusion.177), kind=kCustom, calls=%fused_computation.121 | custom fusion | flops 737280 | bytes 847360 | tf_op jit(solution)/shard_map/scatter-add | solution.py:98
  190.5 18.5 %all-gather.1 = f32[256,20]{1,0:T(8,128)S(1)} all-gather(f32[16,20]{1,0:T(8,128)S(1)} %fusion.49), channel_id=3, replica_groups=mesh['group'=2,'cell'=16] {'cell'}, dimensions={0}, use_global_device_ids=true | all-gather | bytes 21760 | tf_op jit(solution)/shard_map/all_gather | solution.py:39
  214.4 4.4 collective-permute-done.2
  221.4 26.6 %scatter_custom_fusion.4 = f32[80,1280]{0,1:T(8,128)} fusion(s32[3072]{0:T(1024)} %bitcast.285, f32[]{:T(128)} %constant.24.clone.8, f32[3072]{0:T(1024)S(1)} %copy-done.1, pred[3072]{0:T(1024)(128)(4,1)S(1)} %compare_and_fusion, f32[]{:T(128)} %constant.44.clone.1, f32[80,1280]{0,1:T(8,128)S(1)} %fusion.170, s32[3072]{0:T(1024)S(1)} %fusion.178), kind=kCustom, calls=%fused_computation.118 | custom fusion | flops 737280 | bytes 847872 | tf_op jit(solution)/shard_map/scatter-add | solution.py:95
  250.0 27.8 %scatter_custom_fusion.5 = f32[80,1280]{0,1:T(8,128)} fusion(f32[80,1280]{0,1:T(8,128)} %scatter_custom_fusion.4, s32[3072]{0:T(1024)} %bitcast.277, f32[]{:T(128)} %constant.24.clone.8, f32[3072]{0:T(1024)S(1)} %copy-done.1, pred[3072]{0:T(1024)(128)(4,1)S(1)} %compare_and_fusion.1, f32[80,1280]{0,1:T(8,128)S(1)} %fusion.169, s32[3072]{0:T(1024)S(1)} %fusion.177), kind=kCustom, calls=%fused_computation.115 | custom fusion | flops 737280 | bytes 847360 | tf_op jit(solution)/shard_map/scatter-add | solution.py:98
  291.9 37.3 %scatter_custom_fusion.6 = f32[80,1280]{0,1:T(8,128)} fusion(s32[3072]{0:T(1024)} %bitcast.286, f32[]{:T(128)} %constant.24.clone.8, f32[3072]{0:T(1024)S(1)} %copy-done.1, pred[3072]{0:T(1024)(128)(4,1)S(1)} %compare_and_fusion, f32[]{:T(128)} %constant.44.clone.1, f32[80,1280]{0,1:T(8,128)} %fusion.172, s32[3072]{0:T(1024)S(1)} %fusion.178), kind=kCustom, calls=%fused_computation.112 | custom fusion | flops 737280 | bytes 1093632 | tf_op jit(solution)/shard_map/scatter-add | solution.py:95
  331.3 38.6 %scatter_custom_fusion.7 = f32[80,1280]{0,1:T(8,128)} fusion(f32[80,1280]{0,1:T(8,128)} %scatter_custom_fusion.6, s32[3072]{0:T(1024)} %bitcast.278, f32[]{:T(128)} %constant.24.clone.8, f32[3072]{0:T(1024)S(1)} %copy-done.1, pred[3072]{0:T(1024)(128)(4,1)S(1)} %compare_and_fusion.1, f32[80,1280]{0,1:T(8,128)} %fusion.171, s32[3072]{0:T(1024)S(1)} %fusion.177), kind=kCustom, calls=%fused_computation.109 | custom fusion | flops 737280 | bytes 1093120 | tf_op jit(solution)/shard_map/scatter-add | solution.py:98
  387.0 17.5 %all-gather.2 = f32[256,20]{1,0:T(8,128)S(1)} all-gather(f32[16,20]{1,0:T(8,128)S(1)} %fusion.50), channel_id=4, replica_groups=mesh['group'=2,'cell'=16] {'cell'}, dimensions={0}, use_global_device_ids=true | all-gather | bytes 21760 | tf_op jit(solution)/shard_map/all_gather | solution.py:39
  417.5 27.0 %scatter_custom_fusion.8 = f32[80,1280]{0,1:T(8,128)} fusion(s32[3072]{0:T(1024)} %bitcast.287, f32[]{:T(128)} %constant.24.clone.8, f32[3072]{0:T(1024)S(1)} %copy-done.1, pred[3072]{0:T(1024)(128)(4,1)S(1)} %compare_and_fusion, f32[]{:T(128)} %constant.44.clone.1, f32[80,1280]{0,1:T(8,128)S(1)} %fusion.166, s32[3072]{0:T(1024)S(1)} %fusion.178), kind=kCustom, calls=%fused_computation.106 | custom fusion | flops 737280 | bytes 847872 | tf_op jit(solution)/shard_map/scatter-add | solution.py:95
  446.5 27.7 %scatter_custom_fusion.9 = f32[80,1280]{0,1:T(8,128)} fusion(f32[80,1280]{0,1:T(8,128)} %scatter_custom_fusion.8, s32[3072]{0:T(1024)} %bitcast.279, f32[]{:T(128)} %constant.24.clone.8, f32[3072]{0:T(1024)S(1)} %copy-done.1, pred[3072]{0:T(1024)(128)(4,1)S(1)} %compare_and_fusion.1, f32[80,1280]{0,1:T(8,128)S(1)} %fusion.165, s32[3072]{0:T(1024)S(1)} %fusion.177), kind=kCustom, calls=%fused_computation.103 | custom fusion | flops 737280 | bytes 847360 | tf_op jit(solution)/shard_map/scatter-add | solution.py:98
  488.3 37.5 %scatter_custom_fusion.10 = f32[80,1280]{0,1:T(8,128)} fusion(s32[3072]{0:T(1024)} %bitcast.288, f32[]{:T(128)} %constant.24.clone.8, f32[3072]{0:T(1024)S(1)} %copy-done.1, pred[3072]{0:T(1024)(128)(4,1)S(1)} %compare_and_fusion, f32[]{:T(128)} %constant.44.clone.1, f32[80,1280]{0,1:T(8,128)} %fusion.168, s32[3072]{0:T(1024)S(1)} %fusion.178), kind=kCustom, calls=%fused_computation.100 | custom fusion | flops 737280 | bytes 1093632 | tf_op jit(solution)/shard_map/scatter-add | solution.py:95
  527.8 38.4 %scatter_custom_fusion.11 = f32[80,1280]{0,1:T(8,128)} fusion(f32[80,1280]{0,1:T(8,128)} %scatter_custom_fusion.10, s32[3072]{0:T(1024)} %bitcast.280, f32[]{:T(128)} %constant.24.clone.8, f32[3072]{0:T(1024)S(1)} %copy-done.1, pred[3072]{0:T(1024)(128)(4,1)S(1)} %compare_and_fusion.1, f32[80,1280]{0,1:T(8,128)} %fusion.167, s32[3072]{0:T(1024)S(1)} %fusion.177), kind=kCustom, calls=%fused_computation.97 | custom fusion | flops 737280 | bytes 1093120 | tf_op jit(solution)/shard_map/scatter-add | solution.py:98
  583.3 17.5 %all-gather.3 = f32[256,20]{1,0:T(8,128)S(1)} all-gather(f32[16,20]{1,0:T(8,128)S(1)} %fusion.51), channel_id=5, replica_groups=mesh['group'=2,'cell'=16] {'cell'}, dimensions={0}, use_global_device_ids=true | all-gather | bytes 21760 | tf_op jit(solution)/shard_map/all_gather | solution.py:39
  606.6 4.8 collective-permute-done.6
  613.3 26.0 %scatter_custom_fusion.12 = f32[80,1280]{0,1:T(8,128)S(1)} fusion(s32[3072]{0:T(1024)} %bitcast.289, f32[]{:T(128)} %constant.24.clone.8, f32[3072]{0:T(1024)S(1)} %copy-done.1, pred[3072]{0:T(1024)(128)(4,1)S(1)} %compare_and_fusion, f32[]{:T(128)} %constant.44.clone.1, f32[80,1280]{0,1:T(8,128)S(1)} %fusion.162, s32[3072]{0:T(1024)S(1)} %fusion.178), kind=kCustom, calls=%fused_computation.94 | custom fusion | flops 737280 | bytes 847872 | tf_op jit(solution)/shard_map/scatter-add | solution.py:95
  640.5 26.3 %scatter_custom_fusion.13 = f32[80,1280]{0,1:T(8,128)S(1)} fusion(f32[80,1280]{0,1:T(8,128)S(1)} %scatter_custom_fusion.12, s32[3072]{0:T(1024)} %bitcast.281, f32[]{:T(128)} %constant.24.clone.8, f32[3072]{0:T(1024)S(1)} %copy-done.1, pred[3072]{0:T(1024)(128)(4,1)S(1)} %compare_and_fusion.1, f32[80,1280]{0,1:T(8,128)S(1)} %fusion.161, s32[3072]{0:T(1024)S(1)} %fusion.177), kind=kCustom, calls=%fused_computation.91 | custom fusion | flops 737280 | bytes 1093120 | tf_op jit(solution)/shard_map/scatter-add | solution.py:98
  675.6 26.6 %scatter_custom_fusion.14 = f32[80,1280]{0,1:T(8,128)} fusion(s32[3072]{0:T(1024)} %bitcast.290, f32[]{:T(128)} %constant.24.clone.8, f32[3072]{0:T(1024)S(1)} %copy-done.1, pred[3072]{0:T(1024)(128)(4,1)S(1)} %compare_and_fusion, f32[]{:T(128)} %constant.44.clone.1, f32[80,1280]{0,1:T(8,128)S(1)} %fusion.164, s32[3072]{0:T(1024)S(1)} %fusion.178), kind=kCustom, calls=%fused_computation.88 | custom fusion | flops 737280 | bytes 847872 | tf_op jit(solution)/shard_map/scatter-add | solution.py:95
  703.5 27.9 %scatter_custom_fusion.15 = f32[80,1280]{0,1:T(8,128)} fusion(f32[80,1280]{0,1:T(8,128)} %scatter_custom_fusion.14, s32[3072]{0:T(1024)} %bitcast.282, f32[]{:T(128)} %constant.24.clone.8, f32[3072]{0:T(1024)S(1)} %copy-done.1, pred[3072]{0:T(1024)(128)(4,1)S(1)} %compare_and_fusion.1, f32[80,1280]{0,1:T(8,128)S(1)} %fusion.163, s32[3072]{0:T(1024)S(1)} %fusion.177), kind=kCustom, calls=%fused_computation.85 | custom fusion | flops 737280 | bytes 847360 | tf_op jit(solution)/shard_map/scatter-add | solution.py:98
  741.8 17.5 %all-gather.4 = f32[256,20]{1,0:T(8,128)S(1)} all-gather(f32[16,20]{1,0:T(8,128)S(1)} %fusion.52), channel_id=6, replica_groups=mesh['group'=2,'cell'=16] {'cell'}, dimensions={0}, use_global_device_ids=true | all-gather | bytes 21760 | tf_op jit(solution)/shard_map/all_gather | solution.py:39
  (315 shorter events, 177.3 us)
Async XLA Ops:
  0.6 9.1 %copy-start.24 = (s32[2,3072]{1,0:T(2,128)S(1)}, s32[2,3072]{1,0:T(2,128)}, u32[]{:S(2)}) copy-start(s32[2,3072]{1,0:T(2,128)} %param.32) | copy-start | bytes 73732
  0.6 10.0 %copy-start.23 = (f32[16,5,1024]{2,0,1:T(8,128)S(1)}, f32[16,5,1024]{2,0,1:T(8,128)}, u32[]{:S(2)}) copy-start(f32[16,5,1024]{2,0,1:T(8,128)} %param.27) | copy-start | bytes 983044
  2.2 8.7 %copy-start = (f32[20,5,1024]{2,0,1:T(8,128)S(1)}, f32[20,5,1024]{2,0,1:T(8,128)}, u32[]{:S(2)}) copy-start(f32[20,5,1024]{2,0,1:T(8,128)} %param.30) | copy-start | bytes 1228804
  2.9 43.0 %collective-permute-start.1 = (f32[80,128]{1,0:T(8,128)}, f32[80,128]{1,0:T(8,128)S(1)}, u32[]{:S(2)}, u32[]{:S(2)}) collective-permute-start(f32[80,128]{1,0:T(8,128)} %select_bitcast_fusion.6), channel_id=1, source_target_pairs={{0,15},{1,0},{2,1},{3,2},{4,3},{5,4},{6,5},{7,6},{8,7},{9,8},{10,9... | collective-permute-start | bytes 122888 | tf_op jit(solution)/shard_map/ppermute | solution.py:14
  9.7 36.2 %collective-permute-start = (f32[80,128]{1,0:T(8,128)}, f32[80,128]{1,0:T(8,128)S(1)}, u32[]{:S(2)}, u32[]{:S(2)}) collective-permute-start(f32[80,128]{1,0:T(8,128)} %select_bitcast_fusion.7), channel_id=1, source_target_pairs={{0,1},{1,2},{2,3},{3,4},{4,5},{5,6},{6,7},{7,8},{8,9},{9,10},{10,1... | collective-permute-start | bytes 122888 | tf_op jit(solution)/shard_map/ppermute | solution.py:14
  10.8 20.4 %copy-start.38 = (f32[20]{0:T(128)S(1)}, f32[20]{0:T(128)}, u32[]{:S(2)}) copy-start(f32[20]{0:T(128)} %param.31) | copy-start | bytes 244
  185.5 23.5 %copy-start.39 = (f32[20]{0:T(128)S(1)}, f32[20]{0:T(128)}, u32[]{:S(2)}) copy-start(f32[20]{0:T(128)} %param.31) | copy-start | bytes 244
  190.5 21.7 %copy-start.32 = (pred[128]{0:T(512)(128)(4,1)S(1)}, pred[128]{0:T(512)(128)(4,1)}, u32[]{:S(2)}) copy-start(pred[128]{0:T(512)(128)(4,1)} %copy-done.31) | copy-start | bytes 388
  211.2 2.6 collective-permute-start.3
  212.2 6.6 collective-permute-start.2
  289.9 39.4 %copy-start.13 = (f32[80,128]{1,0:T(8,128)S(1)}, f32[80,128]{1,0:T(8,128)}, u32[]{:S(2)}) copy-start(f32[80,128]{1,0:T(8,128)} %copy-done.11) | copy-start | bytes 122884
  289.9 39.4 %copy-start.19 = (f32[80,128]{1,0:T(8,128)S(1)}, f32[80,128]{1,0:T(8,128)}, u32[]{:S(2)}) copy-start(f32[80,128]{1,0:T(8,128)} %copy-done.17) | copy-start | bytes 122884
  382.0 22.5 %copy-start.40 = (f32[20]{0:T(128)S(1)}, f32[20]{0:T(128)}, u32[]{:S(2)}) copy-start(f32[20]{0:T(128)} %param.31) | copy-start | bytes 244
  387.0 21.7 %copy-start.33 = (pred[128]{0:T(512)(128)(4,1)S(1)}, pred[128]{0:T(512)(128)(4,1)}, u32[]{:S(2)}) copy-start(pred[128]{0:T(512)(128)(4,1)} %copy-done.31) | copy-start | bytes 388
  406.7 3.6 collective-permute-start.5
  408.7 6.2 collective-permute-start.4
  486.2 39.5 %copy-start.16 = (f32[80,128]{1,0:T(8,128)S(1)}, f32[80,128]{1,0:T(8,128)}, u32[]{:S(2)}) copy-start(f32[80,128]{1,0:T(8,128)} %copy-done.14) | copy-start | bytes 122884
  486.2 39.5 %copy-start.22 = (f32[80,128]{1,0:T(8,128)S(1)}, f32[80,128]{1,0:T(8,128)}, u32[]{:S(2)}) copy-start(f32[80,128]{1,0:T(8,128)} %copy-done.20) | copy-start | bytes 122884
  578.4 22.5 %copy-start.41 = (f32[20]{0:T(128)S(1)}, f32[20]{0:T(128)}, u32[]{:S(2)}) copy-start(f32[20]{0:T(128)} %param.31) | copy-start | bytes 244
  583.3 21.7 %copy-start.34 = (pred[128]{0:T(512)(128)(4,1)S(1)}, pred[128]{0:T(512)(128)(4,1)}, u32[]{:S(2)}) copy-start(pred[128]{0:T(512)(128)(4,1)} %copy-done.31) | copy-start | bytes 388
  603.0 3.6 collective-permute-start.7
  605.1 6.4 collective-permute-start.6
  613.3 26.0 %copy-start.8 = (f32[80,128]{1,0:T(8,128)S(1)}, f32[80,128]{1,0:T(8,128)}, u32[]{:S(2)}) copy-start(f32[80,128]{1,0:T(8,128)} %copy-done.7) | copy-start | bytes 122884
  613.3 26.0 %copy-start.10 = (f32[80,128]{1,0:T(8,128)S(1)}, f32[80,128]{1,0:T(8,128)}, u32[]{:S(2)}) copy-start(f32[80,128]{1,0:T(8,128)} %copy-done.9) | copy-start | bytes 122884
  (37 other events, 87.0 us)
